TPU v7x, 512 devices: a whole 4x8x8 slice. The times are simulated.
512 devices in a mesh: ctx: 128 (over y, z, core), req: 4 (over x).
Axes of the slice: x: 4, y: 8, z: 8, core: 2. Of those that a mesh axis runs over, the one named last changes fastest.
Arguments:
- queries: bfloat16 [65536, 1024], P(('req', 'ctx')), parts along dimension 0, may hold values from -6 to 6
- keys: bfloat16 [65536, 256], P(('req', 'ctx')), parts along dimension 0, may hold values from -6 to 6
- lse: float32 [16, 65536], P(None, ('req', 'ctx')), parts along dimension 1, may hold values from -0.5 to 15, as said below
- length: int32 [4], P('req'), parts along dimension 0, may hold values from 8192 to 16384
Outputs:
- key_scores: float32 [16, 65536], P(None, ('req', 'ctx')), parts along dimension 1
There are 4 independent parts, one for each index of `req`. A program takes and returns all parts, laid end to end along the dimension named above; each array names one. Nothing has to cross between parts.
Inputs may be any that keep to these rules, and one draw needn't show every extreme that they name: lse[h, i] is the logarithm of i + 1 plus an offset between -0.5 and 3.
All inputs are finite; a program needn't handle non-finite values.
Results may differ from a plain program's by a relative error of at most 0.0003.
Values may be sent and summed in bfloat16 or wider, within the bound.
A program may use at most 64 MiB of HBM per device.

v0:
```python
import functools

import jax
import jax.numpy as jnp
from jax import lax
from jax.experimental import pallas as pl
from jax.experimental.pallas import tpu as pltpu
from jax.sharding import PartitionSpec as P

HEAD_DIM = 64
TOK = 128
NY, NZ = 8, 8
GROUP = 4
PAST = -30000.0
F32, BF16 = jnp.float32, jnp.bfloat16


def member(half, index):
    return 2 * index + (half + index // 2) % 2


def kernel(
    len_ref, q_ref, k_ref, l_ref, o_ref,
    qsend, kpack, kbuf, qbuf, qaug, kaug, acc, part, abuf, ssum, bbuf,
    col_s, col_r, q_s, q_r, relay_s, relay_r, ring_s, ring_r, a_s, a_r, b_s, b_r,
):
    me = lax.axis_index("ctx")
    y, z, c = me // 16, (me // 2) % 8, me % 2
    half, mine = (y + y // 4) % 2, y // 2

    def device(ty, tz, tc):
        return {"ctx": ty * 16 + tz * 2 + tc}

    def remote(src, dst, send, recv, dev):
        return pltpu.make_async_remote_copy(
            src_ref=src, dst_ref=dst, send_sem=send, recv_sem=recv, device_id=dev
        )

    barrier = pltpu.get_barrier_semaphore()

    def greet(dev):
        pl.semaphore_signal(barrier, inc=1, device_id=dev)

    greet(device(y, z, 1 - c))
    for step in range(1, 8):
        greet(device((y + step) % 8, z, c))
        greet(device(y, (z + step) % 8, c))

    lane64 = lax.broadcasted_iota(jnp.int32, (64, TOK), 1)

    for pair in range(2):
        two = k_ref[:, pair * 128 : pair * 128 + 128].astype(F32) * HEAD_DIM**-0.5
        top, low = two[:64], two[64:]
        top_r, low_r = pltpu.roll(top, 64, 1), pltpu.roll(low, 64, 1)
        kpack[2 * pair] = jnp.where(lane64 < 64, top, low_r).astype(BF16)
        kpack[2 * pair + 1] = jnp.where(lane64 < 64, top_r, low).astype(BF16)
    kbuf[z, y] = kpack[mine]

    position = me * TOK + lax.broadcasted_iota(jnp.int32, (16, TOK), 1)
    neg = jnp.where(position < len_ref[0], -l_ref[...], PAST)
    hi = neg.astype(BF16).astype(F32)
    mid = (neg - hi).astype(BF16).astype(F32)
    low = neg - hi - mid
    for head in range(4):
        rows = slice(4 * head, 4 * head + 4)
        parts = jnp.concatenate(
            [hi[rows], mid[rows], low[rows], jnp.zeros((4, TOK), F32)], axis=0
        )
        qsend[head, :TOK, :] = q_ref[:, head * 256 : head * 256 + 256]
        qsend[head, TOK:, :] = jnp.concatenate([parts, parts], axis=1).astype(BF16)

    pl.semaphore_wait(barrier, 15)

    def column(src_y, dst_y):
        return remote(
            kpack.at[dst_y // 2], kbuf.at[z, src_y], col_s.at[dst_y], col_r.at[src_y],
            device(dst_y, z, c),
        )

    def query(src_m, dst_m):
        return remote(
            qsend.at[dst_m], qbuf.at[src_m, c], q_s.at[dst_m], q_r.at[src_m],
            device(member(half, dst_m), z, c),
        )

    def relay(src, m, core):
        return remote(src, qbuf.at[m, core], relay_s.at[m], relay_r.at[m], device(y, z, 1 - c))

    def ring(way, dist, part_of):
        sign = 1 - 2 * way
        block = (z - sign * (dist - 1)) % 8
        where = kbuf.at[block, pl.ds(4 * part_of, 4)]
        return remote(
            where, where, ring_s.at[way, dist - 1, part_of], ring_r.at[way, dist - 1, part_of],
            device(y, (z + sign) % 8, c),
        )

    for step in range(1, 8):
        column(y, (y + step) % 8).start()
    own = relay(qsend.at[mine], mine, c)
    own.start()
    for step in range(1, 4):
        query(mine, (mine + step) % 4).start()
    qbuf[mine, c] = qsend[mine]

    for part_of in range(2):
        for src in range(4 * part_of, 4 * part_of + 4):

            @pl.when(src != y)
            def _():
                column(src, y).wait_recv()

        for way in range(2):
            ring(way, 1, part_of).start()

    def advance(dist):
        for part_of in range(2):
            for way in range(2):
                ring(way, dist, part_of).wait_recv()
                if dist < 3 or part_of == way:
                    ring(way, dist + 1, part_of).start()

    for step in range(1, 4):
        src = (mine - step) % 4
        query(src, mine).wait_recv()
        relay(qbuf.at[src, c], src, c).start()
    advance(1)
    for step in range(4):
        m = (mine - step) % 4
        relay(qbuf.at[m, 1 - c], m, 1 - c).wait_recv()

    lane = lax.broadcasted_iota(jnp.int32, (TOK, TOK), 1)

    def prepare(index, carry):
        m, core = index // 2, index % 2
        tail = qbuf[m, core, TOK:, :TOK].astype(F32)
        cols = jnp.concatenate(
            [jnp.zeros((64, TOK), F32), tail, jnp.zeros((48, TOK), F32)], axis=0
        ).T
        for pair in range(2):
            two = qbuf[m, core, :TOK, pair * 128 : pair * 128 + 128].astype(F32)
            for odd in range(2):
                g = 2 * pair + odd
                head = pltpu.roll(two, 64, 1) if odd else two
                keep = (lane >= 64) & (lane % 4 == g)
                value = jnp.where(lane < 64, head, jnp.where(keep, cols, 0.0))
                qaug[m, g, pl.ds(core * TOK, TOK), :] = value.astype(BF16)
        return carry

    lax.fori_loop(0, 8, prepare, 0)
    advance(2)

    tokens = lax.broadcasted_iota(jnp.int32, (2 * TOK, TOK), 0)
    key_at = lax.broadcasted_iota(jnp.int32, (2 * TOK, TOK), 1) + c * TOK

    def tile(m, start, width, masked=False):
        keys = kaug[pl.ds(start, width), :]
        for g in range(4):
            s = lax.dot_general(
                qaug[m, g], keys, (((1,), (1,)), ((), ())), preferred_element_type=F32
            )
            w = jnp.exp(s)
            if masked:
                w = jnp.where(tokens >= key_at, w, 0.0)
            acc[g, :, pl.ds(start, width)] += jnp.sum(w.reshape(-1, 8, width), axis=0)

    def block_at(turn):
        sign = 1 - 2 * (turn % 2)
        away = jnp.where(turn == 7, 0, (turn // 2 + 1) * sign)
        return (z - away + 8) % 8

    def to_row_mate(block):
        return remote(
            part.at[block], abuf.at[z], a_s.at[block], a_r.at[z], device(y, block, c)
        )

    def one_block(turn, carry):
        block = block_at(turn)

        @pl.when(turn == 3)
        def _():
            advance(3)

        @pl.when(turn == 6)
        def _():
            for way in range(2):
                ring(way, 4, way).wait_recv()

        for src in range(8):
            packed = kbuf[block, src].astype(F32)
            tail = jnp.where(lane64 < 76, 1.0, 0.0)
            kaug[src * TOK : src * TOK + 64, :] = jnp.where(lane64 < 64, packed, tail).astype(BF16)
            kaug[src * TOK + 64 : src * TOK + 128, :] = jnp.where(
                lane64 < 64, pltpu.roll(packed, 64, 1), tail
            ).astype(BF16)
        acc[...] = jnp.zeros_like(acc)
        for m in range(1, 4):
            tile(m, 0, 256 * m)
        odd_m, even_m = 2 * (1 - half), 2 * half

        def at(m, add):
            return pl.multiple_of(256 * m + add, 128)

        @pl.when(block < z)
        def _():
            for i in range(2):
                tile(odd_m + i, at(odd_m + i, 0), 256)
                tile(even_m + i, at(even_m + i, 0), 128)

        @pl.when(block >= z)
        def _():
            for i in range(2):
                tile(odd_m + i, at(odd_m + i, 0), 128)

        @pl.when(block == z)
        def _():
            for i in range(2):
                tile(odd_m + i, at(odd_m + i, 128), 128, masked=True)
                tile(even_m + i, at(even_m + i, 0), 128, masked=True)

        rows = [jnp.sum(acc[g], axis=0, keepdims=True) for g in range(4)]
        part[block] = jnp.concatenate(
            [r[:, :512] for r in rows] + [r[:, 512:] for r in rows], axis=0
        )

        @pl.when(turn < 7)
        def _():
            to_row_mate(block).start()

        return carry

    lax.fori_loop(0, 8, one_block, 0)

    total = part[z]
    for step in range(1, 8):
        src = (z + step) % 8
        remote(part.at[z], abuf.at[src], a_s.at[src], a_r.at[src], device(y, src, c)).wait_recv()
        total += abuf[src]
    for i in range(4):
        ssum[i] = total[:, i * 128 : i * 128 + 128]

    def to_owner(src_y, dst_y):
        return remote(
            ssum.at[dst_y % 4], bbuf.at[src_y], b_s.at[dst_y], b_r.at[src_y],
            device(dst_y, z, c),
        )

    for step in range(1, 8):
        to_owner(y, (y + step) % 8).start()
    bbuf[y] = ssum[y % 4]

    for step in range(1, 8):
        column(y, (y + step) % 8).wait_send()
        to_row_mate((z + step) % 8).wait_send()
    for step in range(1, 4):
        query(mine, (mine + step) % 4).wait_send()
    for m in range(4):
        relay(qbuf.at[m, c], m, c).wait_send()
    for way in range(2):
        for dist in range(1, 5):
            for part_of in range(2):
                if dist < 4 or part_of == way:
                    ring(way, dist, part_of).wait_send()

    for step in range(1, 8):
        to_owner((y + step) % 8, y).wait_recv()
    for h in range(4):
        both = bbuf[2 * h] + bbuf[2 * h + 1]
        o_ref[4 * h : 4 * h + 4, :] = jnp.where(y // 4 == 0, both[:4], both[4:])
    for step in range(1, 8):
        to_owner(y, (y + step) % 8).wait_send()


def shard(queries, keys, lse, length):
    vmem = pl.BlockSpec(memory_space=pltpu.VMEM)
    dma = pltpu.SemaphoreType.DMA
    return pl.pallas_call(
        kernel,
        out_shape=jax.ShapeDtypeStruct(lse.shape, F32),
        in_specs=[pl.BlockSpec(memory_space=pltpu.SMEM), vmem, vmem, vmem],
        out_specs=vmem,
        scratch_shapes=[
            pltpu.VMEM((4, TOK + 16, 256), BF16),
            pltpu.VMEM((4, 64, 128), BF16),
            pltpu.VMEM((NZ, NY, 64, 128), BF16),
            pltpu.VMEM((4, 2, TOK + 16, 256), BF16),
            pltpu.VMEM((4, 4, 2 * TOK, 128), BF16),
            pltpu.VMEM((NY * TOK, 128), BF16),
            pltpu.VMEM((4, 8, NY * TOK), F32),
            pltpu.VMEM((NZ, 8, 512), F32),
            pltpu.VMEM((NZ, 8, 512), F32),
            pltpu.VMEM((4, 8, 128), F32),
            pltpu.VMEM((NY, 8, 128), F32),
            dma((8,)), dma((8,)), dma((4,)), dma((4,)), dma((4,)), dma((4,)),
            dma((2, 4, 2)), dma((2, 4, 2)), dma((8,)), dma((8,)), dma((8,)), dma((8,)),
        ],
        compiler_params=pltpu.CompilerParams(
            collective_id=0, has_side_effects=True, vmem_limit_bytes=48 * 2**20
        ),
    )(length, queries, keys, lse)


def solution(mesh):
    both = ("req", "ctx")
    return jax.shard_map(
        shard,
        mesh=mesh,
        in_specs=(P(both, None), P(both, None), P(None, both), P("req")),
        out_specs=P(None, both),
        check_vma=False,
    )
```

profile of v0, /device:TPU:2, one launch (start us, length us, event | category | flops | bytes accessed | tf_op | source)
XLA Modules:
  0.0 55.4 jit_solution(79145947107769227)
XLA Ops:
  0.7 0.0 copy-start
  0.7 0.9 %copy-done = bf16[128,1024]{1,0:T(8,128)(2,1)S(1)} copy-done((bf16[128,1024]{1,0:T(8,128)(2,1)S(1)}, bf16[128,1024]{1,0:T(8,128)(2,1)}, u32[]{:S(2)}) %copy-start) | copy-done | bytes 262168
  1.6 0.0 copy-start.1
  1.6 0.8 %copy-done.1 = bf16[128,256]{1,0:T(8,128)(2,1)S(1)} copy-done((bf16[128,256]{1,0:T(8,128)(2,1)S(1)}, bf16[128,256]{1,0:T(8,128)(2,1)}, u32[]{:S(2)}) %copy-start.1) | copy-done | bytes 65560
  2.4 0.0 copy-start.2
  2.4 0.7 %copy-done.2 = f32[16,128]{1,0:T(8,128)S(1)} copy-done((f32[16,128]{1,0:T(8,128)S(1)}, f32[16,128]{1,0:T(8,128)}, u32[]{:S(2)}) %copy-start.2) | copy-done | bytes 8216
  3.1 51.7 %shard_map.46 = f32[16,128]{1,0:T(8,128)S(1)} custom-call(s32[1]{0:T(128)S(6)} %copy.6.len_ref, bf16[128,1024]{1,0:T(8,128)(2,1)S(1)} %copy-done, bf16[128,256]{1,0:T(8,128)(2,1)S(1)} %copy-done.1, f32[16,128]{1,0:T(8,128)S(1)} %copy-done.2), custom_call_target="tpu_custom_call" | custom-call | tf_op jit(solution)/shard_map/pallas_call | solution.py:277
  54.8 0.6 %copy.7 = f32[16,128]{1,0:T(8,128)} copy(f32[16,128]{1,0:T(8,128)S(1)} %shard_map.46) | data formatting | bytes 16384
Async XLA Ops:
  0.7 1.0 %copy-start = (bf16[128,1024]{1,0:T(8,128)(2,1)S(1)}, bf16[128,1024]{1,0:T(8,128)(2,1)}, u32[]{:S(2)}) copy-start(bf16[128,1024]{1,0:T(8,128)(2,1)} %q_ref.1) | copy-start | bytes 786436
  1.6 0.8 %copy-start.1 = (bf16[128,256]{1,0:T(8,128)(2,1)S(1)}, bf16[128,256]{1,0:T(8,128)(2,1)}, u32[]{:S(2)}) copy-start(bf16[128,256]{1,0:T(8,128)(2,1)} %k_ref.1) | copy-start | bytes 196612
  2.4 0.7 %copy-start.2 = (f32[16,128]{1,0:T(8,128)S(1)}, f32[16,128]{1,0:T(8,128)}, u32[]{:S(2)}) copy-start(f32[16,128]{1,0:T(8,128)} %l_ref.1) | copy-start | bytes 24580
where the time goes:
time: 55.7 us; the launch traced here: 55.4 us
  Pallas kernels  51.7 us (93%)
  local copies, waits for them, and re-layouts  3.08 us (6%)
  between operations  0.67 us (1%)
    pallas_call x1, Pallas kernels, shard(): pl.pallas_call(kernel, out_shape=jax.ShapeDtypeStruct(lse.shape, F32), in...  51.7 us
    unnamed x7, local copies, waits for them, and re-layouts  3.08 us

commit v1 on v0

v1 whole, which is shorter than its diff:
```python
import functools

import jax
import jax.numpy as jnp
from jax import lax
from jax.experimental import pallas as pl
from jax.experimental.pallas import tpu as pltpu
from jax.sharding import PartitionSpec as P

HEAD_DIM = 64
TOK = 128
NY, NZ = 8, 8
GROUP = 4
PAST = -30000.0
F32, BF16 = jnp.float32, jnp.bfloat16


def member(half, index):
    return 2 * index + (half + index // 2) % 2


def kernel(
    len_ref, q_hbm, k_hbm, l_hbm, o_ref,
    q_ref, k_ref, l_ref, qsend, kpack, kbuf, qbuf, qaug, kaug, acc, part, abuf,
    in_s, col_s, col_r, q_s, q_r, relay_s, relay_r, ring_s, ring_r, a_s, a_r,
):
    me = lax.axis_index("ctx")
    y, z, c = me // 16, (me // 2) % 8, me % 2
    half, mine = (y + y // 4) % 2, y // 2

    def device(ty, tz, tc):
        return {"ctx": ty * 16 + tz * 2 + tc}

    def remote(src, dst, send, recv, dev):
        return pltpu.make_async_remote_copy(
            src_ref=src, dst_ref=dst, send_sem=send, recv_sem=recv, device_id=dev
        )

    loads = [
        pltpu.make_async_copy(src, dst, in_s.at[i])
        for i, (src, dst) in enumerate(((k_hbm, k_ref), (l_hbm, l_ref), (q_hbm, q_ref)))
    ]
    for load in loads:
        load.start()
    barrier = pltpu.get_barrier_semaphore()

    def greet(dev):
        pl.semaphore_signal(barrier, inc=1, device_id=dev)

    greet(device(y, z, 1 - c))
    for step in range(1, 8):
        greet(device((y + step) % 8, z, c))
        greet(device(y, (z + step) % 8, c))

    lane64 = lax.broadcasted_iota(jnp.int32, (64, TOK), 1)

    for load in loads:
        load.wait()

    for pair in range(2):
        two = k_ref[:, pair * 128 : pair * 128 + 128].astype(F32) * HEAD_DIM**-0.5
        top, low = two[:64], two[64:]
        top_r, low_r = pltpu.roll(top, 64, 1), pltpu.roll(low, 64, 1)
        kpack[2 * pair] = jnp.where(lane64 < 64, top, low_r).astype(BF16)
        kpack[2 * pair + 1] = jnp.where(lane64 < 64, top_r, low).astype(BF16)
    kbuf[z, y] = kpack[mine]

    position = me * TOK + lax.broadcasted_iota(jnp.int32, (16, TOK), 1)
    neg = jnp.where(position < len_ref[0], -l_ref[...], PAST)
    hi = neg.astype(BF16).astype(F32)
    mid = (neg - hi).astype(BF16).astype(F32)
    low = neg - hi - mid
    for head in range(4):
        rows = slice(4 * head, 4 * head + 4)
        parts = jnp.concatenate(
            [hi[rows], mid[rows], low[rows], jnp.zeros((4, TOK), F32)], axis=0
        )
        qsend[head, :TOK, :] = q_ref[:, head * 256 : head * 256 + 256]
        qsend[head, TOK:, :] = jnp.concatenate([parts, parts], axis=1).astype(BF16)

    pl.semaphore_wait(barrier, 15)

    def column(src_y, dst_y):
        return remote(
            kpack.at[dst_y // 2], kbuf.at[z, src_y], col_s.at[dst_y], col_r.at[src_y],
            device(dst_y, z, c),
        )

    def query(src_m, dst_m):
        return remote(
            qsend.at[dst_m], qbuf.at[src_m, c], q_s.at[dst_m], q_r.at[src_m],
            device(member(half, dst_m), z, c),
        )

    def relay(src, m, core):
        return remote(src, qbuf.at[m, core], relay_s.at[m], relay_r.at[m], device(y, z, 1 - c))

    def ring(way, dist, part_of):
        sign = 1 - 2 * way
        from_dist, hop = (2, 2) if dist == 4 else (dist - 1, 1)
        block = (z - sign * from_dist) % 8
        where = kbuf.at[block, pl.ds(4 * part_of, 4)]
        return remote(
            where, where, ring_s.at[way, dist - 1, part_of], ring_r.at[way, dist - 1, part_of],
            device(y, (z + hop * sign) % 8, c),
        )

    for step in range(1, 8):
        column(y, (y + step) % 8).start()
    own = relay(qsend.at[mine], mine, c)
    own.start()
    for step in range(1, 4):
        query(mine, (mine + step) % 4).start()
    qbuf[mine, c] = qsend[mine]

    for part_of in range(2):
        for src in range(4 * part_of, 4 * part_of + 4):

            @pl.when(src != y)
            def _():
                column(src, y).wait_recv()

        for way in range(2):
            ring(way, 1, part_of).start()

    def advance(dist):
        for part_of in range(2):
            for way in range(2):
                if dist < 4 or part_of == way:
                    ring(way, dist, part_of).wait_recv()
                if dist < 3:
                    ring(way, dist + 1, part_of).start()
                if dist == 2 and part_of == way:
                    ring(way, 4, part_of).start()

    lane = lax.broadcasted_iota(jnp.int32, (TOK, TOK), 1)

    def prepare(m, core):
        tail = qbuf[m, core, TOK:, :TOK].astype(F32)
        cols = jnp.concatenate(
            [jnp.zeros((64, TOK), F32), tail, jnp.zeros((48, TOK), F32)], axis=0
        ).T
        for pair in range(2):
            two = qbuf[m, core, :TOK, pair * 128 : pair * 128 + 128].astype(F32)
            for odd in range(2):
                g = 2 * pair + odd
                head = pltpu.roll(two, 64, 1) if odd else two
                keep = (lane >= 64) & (lane % 4 == g)
                value = jnp.where(lane < 64, head, jnp.where(keep, cols, 0.0))
                qaug[m, g, pl.ds(core * TOK, TOK), :] = value.astype(BF16)

    prepare(mine, c)
    relay(qbuf.at[mine, 1 - c], mine, 1 - c).wait_recv()
    prepare(mine, 1 - c)
    for step in range(1, 4):
        src = (mine - step) % 4
        query(src, mine).wait_recv()
        relay(qbuf.at[src, c], src, c).start()
        prepare(src, c)
    advance(1)
    for step in range(1, 4):
        src = (mine - step) % 4
        relay(qbuf.at[src, 1 - c], src, 1 - c).wait_recv()
        prepare(src, 1 - c)

    tokens = lax.broadcasted_iota(jnp.int32, (2 * TOK, 2 * TOK), 0)
    key_of = lax.broadcasted_iota(jnp.int32, (1, 2 * TOK), 1)

    def compute(block):
        for src in range(8):
            packed = kbuf[block, src].astype(F32)
            tail = jnp.where(lane64 < 76, 1.0, 0.0)
            at = src * TOK
            kaug[at : at + 64, :] = jnp.where(lane64 < 64, packed, tail).astype(BF16)
            kaug[at + 64 : at + 128, :] = jnp.where(
                lane64 < 64, pltpu.roll(packed, 64, 1), tail
            ).astype(BF16)
        for m in range(3, -1, -1):
            width = 256 * (m + 1)
            key_at = ((2 * m + key_of // TOK) * NZ + block) * 2 * TOK + c * TOK + key_of % TOK
            first = key_at - (member(half, m) * NZ + z) * 2 * TOK
            for g in range(4):
                w = jnp.exp(
                    lax.dot_general(
                        qaug[m, g], kaug[:width, :], (((1,), (1,)), ((), ())),
                        preferred_element_type=F32,
                    )
                )
                seen = jnp.where(tokens >= first, w[:, width - 256 :], 0.0)
                last = jnp.sum(seen.reshape(-1, 8, 256), axis=0)
                if m == 3:
                    acc[g, :, width - 256 : width] = last
                else:
                    acc[g, :, width - 256 : width] += last
                if m > 0:
                    full = jnp.sum(w[:, : width - 256].reshape(-1, 8, width - 256), axis=0)
                    if m == 3:
                        acc[g, :, : width - 256] = full
                    else:
                        acc[g, :, : width - 256] += full
        rows = [jnp.sum(acc[g], axis=0, keepdims=True) for g in range(4)]
        four = jnp.concatenate(rows, axis=0)
        for src in range(8):
            part[block, src] = four[:, src * TOK : src * TOK + TOK]

    def to_owner(block, row):
        return remote(
            part.at[block, row], abuf.at[z * 8 + y], a_s.at[0], a_r.at[0], device(row, block, c)
        )

    def one_block(turn, carry):
        @pl.when(turn == 1)
        def _():
            advance(2)

        @pl.when(turn == 4)
        def _():
            advance(3)

        @pl.when(turn == 6)
        def _():
            advance(4)

        away = jnp.where(turn == 7, -1, (turn // 2 + 1) * (1 - 2 * (turn % 2)))
        away = jnp.where(turn < 2, turn, away)
        block = (z - away + 8) % 8
        compute(block)

        for row in range(8):

            @pl.when((turn > 0) | (row != y))
            def _():
                to_owner(block, row).start()

        return carry

    lax.fori_loop(0, 8, one_block, 0)

    abuf[z * 8 + y] = part[z, y]

    for step in range(1, 8):
        column(y, (y + step) % 8).wait_send()
    for step in range(1, 4):
        query(mine, (mine + step) % 4).wait_send()
    for m in range(4):
        relay(qbuf.at[m, c], m, c).wait_send()
    for way in range(2):
        for dist in range(1, 5):
            for part_of in range(2):
                if dist < 4 or part_of == way:
                    ring(way, dist, part_of).wait_send()

    others = remote(
        abuf.at[pl.ds(0, 63)], abuf.at[pl.ds(0, 63)], a_s.at[0], a_r.at[0], device(y, z, 1 - c)
    )
    others.wait_recv()
    for h in range(4):
        total = abuf[2 * h] + abuf[2 * h + 1]
        for col in range(1, 8):
            total += abuf[8 * col + 2 * h] + abuf[8 * col + 2 * h + 1]
        o_ref[4 * h : 4 * h + 4, :] = total
    others.wait_send()


def shard(queries, keys, lse, length):
    vmem = pl.BlockSpec(memory_space=pltpu.VMEM)
    dma = pltpu.SemaphoreType.DMA
    return pl.pallas_call(
        kernel,
        out_shape=jax.ShapeDtypeStruct(lse.shape, F32),
        in_specs=[pl.BlockSpec(memory_space=pltpu.SMEM)] + [pl.BlockSpec(memory_space=pl.ANY)] * 3,
        out_specs=vmem,
        scratch_shapes=[
            pltpu.VMEM(queries.shape, BF16),
            pltpu.VMEM(keys.shape, BF16),
            pltpu.VMEM(lse.shape, F32),
            pltpu.VMEM((4, TOK + 16, 256), BF16),
            pltpu.VMEM((4, 64, 128), BF16),
            pltpu.VMEM((NZ, NY, 64, 128), BF16),
            pltpu.VMEM((4, 2, TOK + 16, 256), BF16),
            pltpu.VMEM((4, 4, 2 * TOK, 128), BF16),
            pltpu.VMEM((NY * TOK, 128), BF16),
            pltpu.VMEM((4, 8, NY * TOK), F32),
            pltpu.VMEM((NZ, NY, 4, TOK), F32),
            pltpu.VMEM((NZ * NY, 4, TOK), F32),
            dma((3,)), dma((8,)), dma((8,)), dma((4,)), dma((4,)), dma((4,)), dma((4,)),
            dma((2, 4, 2)), dma((2, 4, 2)), dma((1,)), dma((1,)),
        ],
        compiler_params=pltpu.CompilerParams(
            collective_id=0, has_side_effects=True, vmem_limit_bytes=55224 * 1024
        ),
    )(length, queries, keys, lse)


def solution(mesh):
    both = ("req", "ctx")
    return jax.shard_map(
        shard,
        mesh=mesh,
        in_specs=(P(both, None), P(both, None), P(None, both), P("req")),
        out_specs=P(None, both),
        check_vma=False,
    )
```

time: 55.7 us -> 53.8 us (0.966)
  the two profiles are of different devices: /device:TPU:2 before, /device:TPU:4 now
where the time goes in v1:
time: 53.8 us; the launch traced here: 53.7 us
  Pallas kernels  52.4 us (97%)
  between operations  0.66 us (1%)
  local copies, waits for them, and re-layouts  0.6 us (1%)
    pallas_call x1, Pallas kernels, shard(): pl.pallas_call(kernel, out_shape=jax.ShapeDtypeStruct(lse.shape, F32), in...  52.4 us

profile of v1, /device:TPU:4, one launch (start us, length us, event | category | flops | bytes accessed | tf_op | source)
XLA Modules:
  0.0 53.7 jit_solution(16325349083351149085)
XLA Ops:
  0.7 52.4 %shard_map.46 = f32[16,128]{1,0:T(8,128)S(1)} custom-call(s32[1]{0:T(128)S(6)} %copy.6.len_ref, bf16[128,1024]{1,0:T(8,128)(2,1)} %q_hbm.1, bf16[128,256]{1,0:T(8,128)(2,1)} %k_hbm.1, f32[16,128]{1,0:T(8,128)} %l_hbm.1), custom_call_target="tpu_custom_call" | custom-call | tf_op jit(solution)/shard_map/pallas_call | solution.py:268
  53.1 0.6 %copy.7 = f32[16,128]{1,0:T(8,128)} copy(f32[16,128]{1,0:T(8,128)S(1)} %shard_map.46) | data formatting | bytes 16384

commit v2 on v1

--- a/solution.py
+++ b/solution.py
@@ -22,7 +22,7 @@
 def kernel(
     len_ref, q_hbm, k_hbm, l_hbm, o_ref,
     q_ref, k_ref, l_ref, qsend, kpack, kbuf, qbuf, qaug, kaug, acc, part, abuf,
-    in_s, col_s, col_r, q_s, q_r, relay_s, relay_r, ring_s, ring_r, a_s, a_r,
+    in_s, col_s, col_r, q_s, q_r, relay_s, relay_r, ring_s, ring_r, a_s, a_r, right_ok, left_ok,
 ):
     me = lax.axis_index("ctx")
     y, z, c = me // 16, (me // 2) % 8, me % 2
@@ -48,14 +48,20 @@
         pl.semaphore_signal(barrier, inc=1, device_id=dev)
 
     greet(device(y, z, 1 - c))
-    for step in range(1, 8):
+    for step in (4, 3, 5, 2, 6, 1, 7):
         greet(device((y + step) % 8, z, c))
-        greet(device(y, (z + step) % 8, c))
+
+    @pl.when(z < 7)
+    def _():
+        greet(device(y, z + 1, c))
+
+    @pl.when(z == 0)
+    def _():
+        greet(device(y, 7, c))
 
     lane64 = lax.broadcasted_iota(jnp.int32, (64, TOK), 1)
 
-    for load in loads:
-        load.wait()
+    loads[0].wait()
 
     for pair in range(2):
         two = k_ref[:, pair * 128 : pair * 128 + 128].astype(F32) * HEAD_DIM**-0.5
@@ -65,6 +71,45 @@
         kpack[2 * pair + 1] = jnp.where(lane64 < 64, top_r, low).astype(BF16)
     kbuf[z, y] = kpack[mine]
 
+    pl.semaphore_wait(barrier, 8 + jnp.where(z > 0, 1, 0) + jnp.where(z == 7, 1, 0))
+
+    @pl.when(z > 0)
+    def _():
+        pl.semaphore_signal(right_ok, inc=1, device_id=device(y, z - 1, c))
+
+    @pl.when(z == 7)
+    def _():
+        pl.semaphore_signal(left_ok, inc=1, device_id=device(y, 0, c))
+
+    def column(src_y, dst_y):
+        return remote(
+            kpack.at[dst_y // 2], kbuf.at[z, src_y], col_s.at[dst_y], col_r.at[src_y],
+            device(dst_y, z, c),
+        )
+
+    def query(src_m, dst_m):
+        return remote(
+            qsend.at[dst_m], qbuf.at[src_m, c], q_s.at[dst_m], q_r.at[src_m],
+            device(member(half, dst_m), z, c),
+        )
+
+    def relay(src, m, core):
+        return remote(src, qbuf.at[m, core], relay_s.at[m], relay_r.at[m], device(y, z, 1 - c))
+
+    def ring(way, dist, part_of):
+        sign = 1 - 2 * way
+        from_dist, hop = (2, 2) if dist == 4 else (dist - 1, 1)
+        block = (z - sign * from_dist) % 8
+        where = kbuf.at[block, pl.ds(4 * part_of, 4)]
+        return remote(
+            where, where, ring_s.at[way, dist - 1, part_of], ring_r.at[way, dist - 1, part_of],
+            device(y, (z + hop * sign) % 8, c),
+        )
+
+    for step in (4, 3, 5, 2, 6, 1, 7):
+        column(y, (y + step) % 8).start()
+    loads[1].wait()
+    loads[2].wait()
     position = me * TOK + lax.broadcasted_iota(jnp.int32, (16, TOK), 1)
     neg = jnp.where(position < len_ref[0], -l_ref[...], PAST)
     hi = neg.astype(BF16).astype(F32)
@@ -78,35 +123,6 @@
         qsend[head, :TOK, :] = q_ref[:, head * 256 : head * 256 + 256]
         qsend[head, TOK:, :] = jnp.concatenate([parts, parts], axis=1).astype(BF16)
 
-    pl.semaphore_wait(barrier, 15)
-
-    def column(src_y, dst_y):
-        return remote(
-            kpack.at[dst_y // 2], kbuf.at[z, src_y], col_s.at[dst_y], col_r.at[src_y],
-            device(dst_y, z, c),
-        )
-
-    def query(src_m, dst_m):
-        return remote(
-            qsend.at[dst_m], qbuf.at[src_m, c], q_s.at[dst_m], q_r.at[src_m],
-            device(member(half, dst_m), z, c),
-        )
-
-    def relay(src, m, core):
-        return remote(src, qbuf.at[m, core], relay_s.at[m], relay_r.at[m], device(y, z, 1 - c))
-
-    def ring(way, dist, part_of):
-        sign = 1 - 2 * way
-        from_dist, hop = (2, 2) if dist == 4 else (dist - 1, 1)
-        block = (z - sign * from_dist) % 8
-        where = kbuf.at[block, pl.ds(4 * part_of, 4)]
-        return remote(
-            where, where, ring_s.at[way, dist - 1, part_of], ring_r.at[way, dist - 1, part_of],
-            device(y, (z + hop * sign) % 8, c),
-        )
-
-    for step in range(1, 8):
-        column(y, (y + step) % 8).start()
     own = relay(qsend.at[mine], mine, c)
     own.start()
     for step in range(1, 4):
@@ -120,14 +136,27 @@
             def _():
                 column(src, y).wait_recv()
 
-        for way in range(2):
-            ring(way, 1, part_of).start()
+        if part_of == 0:
+
+            @pl.when(z < 7)
+            def _():
+                pl.semaphore_wait(right_ok, 1)
+
+        ring(0, 1, part_of).start()
+
+    @pl.when(z == 0)
+    def _():
+        pl.semaphore_wait(left_ok, 1)
+
+    for part_of in range(2):
+        ring(1, 1, part_of).start()
 
     def advance(dist):
         for part_of in range(2):
             for way in range(2):
                 if dist < 4 or part_of == way:
                     ring(way, dist, part_of).wait_recv()
+            for way in range(2):
                 if dist < 3:
                     ring(way, dist + 1, part_of).start()
                 if dist == 2 and part_of == way:
@@ -152,12 +181,12 @@
     prepare(mine, c)
     relay(qbuf.at[mine, 1 - c], mine, 1 - c).wait_recv()
     prepare(mine, 1 - c)
+    advance(1)
     for step in range(1, 4):
         src = (mine - step) % 4
         query(src, mine).wait_recv()
         relay(qbuf.at[src, c], src, c).start()
         prepare(src, c)
-    advance(1)
     for step in range(1, 4):
         src = (mine - step) % 4
         relay(qbuf.at[src, 1 - c], src, 1 - c).wait_recv()
@@ -213,16 +242,13 @@
         def _():
             advance(2)
 
-        @pl.when(turn == 4)
-        def _():
-            advance(3)
-
-        @pl.when(turn == 6)
+        @pl.when(turn == 5)
         def _():
             advance(4)
-
-        away = jnp.where(turn == 7, -1, (turn // 2 + 1) * (1 - 2 * (turn % 2)))
-        away = jnp.where(turn < 2, turn, away)
+            advance(3)
+
+        away = ((turn + 1) // 2) * (2 * (turn % 2) - 1)
+        away = jnp.where(turn < 5, away, jnp.where(turn == 5, 4, 3 - 6 * (turn - 6)))
         block = (z - away + 8) % 8
         compute(block)
 
@@ -285,6 +311,7 @@
             pltpu.VMEM((NZ * NY, 4, TOK), F32),
             dma((3,)), dma((8,)), dma((8,)), dma((4,)), dma((4,)), dma((4,)), dma((4,)),
             dma((2, 4, 2)), dma((2, 4, 2)), dma((1,)), dma((1,)),
+            pltpu.SemaphoreType.REGULAR, pltpu.SemaphoreType.REGULAR,
         ],
         compiler_params=pltpu.CompilerParams(
             collective_id=0, has_side_effects=True, vmem_limit_bytes=55224 * 1024

time: 53.8 us -> 49.8 us (0.926)
  the two profiles are of different devices: /device:TPU:4 before, /device:TPU:1 now
where the time goes in v2:
time: 49.8 us; the launch traced here: 49.7 us
  Pallas kernels  48.5 us (97%)
  between operations  0.66 us (1%)
  local copies, waits for them, and re-layouts  0.6 us (1%)
    pallas_call x1, Pallas kernels, shard(): pl.pallas_call(kernel, out_shape=jax.ShapeDtypeStruct(lse.shape, F32), in...  48.5 us

profile of v2, /device:TPU:1, one launch (start us, length us, event | category | flops | bytes accessed | tf_op | source)
XLA Modules:
  0.0 49.7 jit_solution(5643920083264267956)
XLA Ops:
  0.7 48.5 %shard_map.46 = f32[16,128]{1,0:T(8,128)S(1)} custom-call(s32[1]{0:T(128)S(6)} %copy.6.len_ref, bf16[128,1024]{1,0:T(8,128)(2,1)} %q_hbm.1, bf16[128,256]{1,0:T(8,128)(2,1)} %k_hbm.1, f32[16,128]{1,0:T(8,128)} %l_hbm.1), custom_call_target="tpu_custom_call" | custom-call | tf_op jit(solution)/shard_map/pallas_call | solution.py:294
  49.1 0.6 %copy.7 = f32[16,128]{1,0:T(8,128)} copy(f32[16,128]{1,0:T(8,128)S(1)} %shard_map.46) | data formatting | bytes 16384

commit v3 on v2

--- a/solution.py
+++ b/solution.py
@@ -195,7 +195,7 @@
     tokens = lax.broadcasted_iota(jnp.int32, (2 * TOK, 2 * TOK), 0)
     key_of = lax.broadcasted_iota(jnp.int32, (1, 2 * TOK), 1)
 
-    def compute(block):
+    def compute(block, own):
         for src in range(8):
             packed = kbuf[block, src].astype(F32)
             tail = jnp.where(lane64 < 76, 1.0, 0.0)
@@ -215,8 +215,12 @@
                         preferred_element_type=F32,
                     )
                 )
-                seen = jnp.where(tokens >= first, w[:, width - 256 :], 0.0)
-                last = jnp.sum(seen.reshape(-1, 8, 256), axis=0)
+                last = w[:, width - 256 :]
+                if own:
+                    last = jnp.where(tokens >= first, last, 0.0)
+                last = jnp.sum(last.reshape(-1, 8, 256), axis=0)
+                if not own:
+                    last = jnp.where(first <= 0, last, 0.0)
                 if m == 3:
                     acc[g, :, width - 256 : width] = last
                 else:
@@ -250,17 +254,17 @@
         away = ((turn + 1) // 2) * (2 * (turn % 2) - 1)
         away = jnp.where(turn < 5, away, jnp.where(turn == 5, 4, 3 - 6 * (turn - 6)))
         block = (z - away + 8) % 8
-        compute(block)
+        compute(block, False)
 
         for row in range(8):
-
-            @pl.when((turn > 0) | (row != y))
-            def _():
-                to_owner(block, row).start()
+            to_owner(block, row).start()
 
         return carry
 
-    lax.fori_loop(0, 8, one_block, 0)
+    compute(z, True)
+    for step in range(1, 8):
+        to_owner(z, (y + step) % 8).start()
+    lax.fori_loop(1, 8, one_block, 0)
 
     abuf[z * 8 + y] = part[z, y]
 

time: 49.8 us -> 49.4 us (level); the launches traced: 49.7 us -> 48.8 us
  Pallas kernels: 48.5 us -> 47.5 us
    pallas_call x1, Pallas kernels: 48.5 us -> 47.5 us  [shard(): pl.pallas_call(kernel, out_shape=jax.ShapeDtypeStruct(lse.shape, F32), in...]
where the time goes in v3:
time: 49.4 us; the launch traced here: 48.8 us
  Pallas kernels  47.5 us (96%)
  between operations  0.66 us (1%)
  local copies, waits for them, and re-layouts  0.6 us (1%)
    pallas_call x1, Pallas kernels, shard(): pl.pallas_call(kernel, out_shape=jax.ShapeDtypeStruct(lse.shape, F32), in...  47.5 us

profile of v3, /device:TPU:1, one launch (start us, length us, event | category | flops | bytes accessed | tf_op | source)
XLA Modules:
  0.0 48.8 jit_solution(15148611911523937946)
XLA Ops:
  0.7 47.5 %shard_map.46 = f32[16,128]{1,0:T(8,128)S(1)} custom-call(s32[1]{0:T(128)S(6)} %copy.6.len_ref, bf16[128,1024]{1,0:T(8,128)(2,1)} %q_hbm.1, bf16[128,256]{1,0:T(8,128)(2,1)} %k_hbm.1, f32[16,128]{1,0:T(8,128)} %l_hbm.1), custom_call_target="tpu_custom_call" | custom-call | tf_op jit(solution)/shard_map/pallas_call | solution.py:298
  48.2 0.6 %copy.7 = f32[16,128]{1,0:T(8,128)} copy(f32[16,128]{1,0:T(8,128)S(1)} %shard_map.46) | data formatting | bytes 16384
